TPU v7x, 128 devices: a whole 4x4x4 slice. The times are simulated.
128 devices in a mesh: ctx: 32 (over z, y_lo, x), kv: 4 (over y_hi, core).
Axes of the slice: x: 4, y: 4 (y_hi: 2, y_lo: 2; y = y_hi * 2 + y_lo), z: 4, core: 2. Of those that a mesh axis runs over, the one named last changes fastest.
Arguments:
- queries: bfloat16 [16384, 4096], P('ctx', 'kv'), may hold values from -6 to 6
- keys: bfloat16 [16384, 1024], P('ctx', 'kv'), may hold values from -6 to 6
- values: bfloat16 [16384, 1024], P('ctx', 'kv'), may hold values from -24 to 24
- doc_lengths: int32 [16], replicated, may hold values from 1 to 12288, 16384 in all
- out_weight: bfloat16 [4096, 4096], P('kv'), may hold values from -0.375 to 0.375
Outputs:
- output: bfloat16 [16384, 4096], P(('ctx', 'kv'))
Inputs may be any that keep to these rules, and one draw needn't show every extreme that they name: `doc_lengths`: whole documents laid end to end that fill all 16384 positions; the longest has exactly 12288 tokens.
All inputs are finite; a program needn't handle non-finite values.
Results may differ from a plain program's by a relative error of at most 0.015.
Values may be sent and summed in bfloat16 or wider, within the bound.
No kernel may reach another device: no remote copies, remote signals or barrier semaphores. Data moves between devices by JAX's collectives and lax.ppermute only.
A program may use at most 192 MiB of HBM per device.

v0:
```python
import math

import jax
import jax.numpy as jnp
from jax import lax
from jax.sharding import PartitionSpec as P

QUERY_HEADS = 32
KEY_VALUE_HEADS = 8
HEAD_WIDTH = 128


NEG_FILL = -1e30


def segment_ids(doc_ends, positions):
    return jnp.sum((doc_ends[None, :] <= positions[:, None]).astype(jnp.int32), axis=1)


def block_update(
    softmax_state,
    query_block,
    query_pos,
    query_seg,
    key_block,
    value_block,
    key_pos,
    key_seg,
    score_scale,
):
    running_max, running_sum, accum = softmax_state
    scores = (
        jnp.einsum("qhgd,khd->hgqk", query_block, key_block, preferred_element_type=jnp.float32)
        * score_scale
    )
    allowed = (key_seg[None, :] == query_seg[:, None]) & (key_pos[None, :] <= query_pos[:, None])
    scores = jnp.where(allowed, scores, NEG_FILL)
    new_max = jnp.maximum(running_max, jnp.max(scores, axis=-1))
    shrink = jnp.exp(running_max - new_max)
    weights = jnp.where(allowed, jnp.exp(scores - new_max[..., None]), 0.0)
    new_sum = running_sum * shrink + jnp.sum(weights, axis=-1)
    rounded = weights.astype(jnp.bfloat16)
    contrib = jnp.einsum("hgqk,khd->qhgd", rounded, value_block, preferred_element_type=jnp.float32)
    new_accum = accum * jnp.transpose(shrink, (2, 0, 1))[..., None] + contrib
    return (new_max, new_sum, new_accum)


def on_device(queries, keys, values, doc_lengths, out_weight):
    my_index = lax.axis_index("ctx")
    shard_rows = queries.shape[0]
    half_rows = shard_rows // 2
    head_local = keys.shape[1] // HEAD_WIDTH
    group_width = QUERY_HEADS // KEY_VALUE_HEADS
    score_scale = HEAD_WIDTH ** (-0.5)
    doc_ends = jnp.cumsum(doc_lengths)
    local_rows = jnp.arange(half_rows, dtype=jnp.int32)
    first_pos = my_index * shard_rows + local_rows
    second_queries = queries[half_rows:]
    second_pos = my_index * shard_rows + half_rows + local_rows
    query_sets = (
        queries[:half_rows].reshape(half_rows, head_local, group_width, HEAD_WIDTH),
        second_queries.reshape(half_rows, head_local, group_width, HEAD_WIDTH),
    )
    pos_sets = (first_pos, second_pos)
    seg_sets = (segment_ids(doc_ends, first_pos), segment_ids(doc_ends, second_pos))

    def fresh_state():
        return (
            jnp.full((head_local, group_width, half_rows), NEG_FILL, jnp.float32),
            jnp.zeros((head_local, group_width, half_rows), jnp.float32),
            jnp.zeros((half_rows, head_local, group_width, HEAD_WIDTH), jnp.float32),
        )

    carry_state = (fresh_state(), fresh_state())
    key_piece = lax.all_gather(keys, "ctx", axis=0, tiled=True)
    value_piece = lax.all_gather(values, "ctx", axis=0, tiled=True)
    row_count = key_piece.shape[0]
    key_width = math.gcd(row_count, 512)
    blocks = row_count // key_width
    key_blocks = key_piece.reshape(blocks, key_width, head_local, HEAD_WIDTH)
    value_blocks = value_piece.reshape(blocks, key_width, head_local, HEAD_WIDTH)
    key_positions = jnp.arange(row_count, dtype=jnp.int32)
    key_segments = segment_ids(doc_ends, key_positions).reshape(blocks, key_width)
    key_positions = key_positions.reshape(blocks, key_width)
    updated = []
    for which in range(2):
        query_block = query_sets[which]
        query_pos = pos_sets[which]
        query_seg = seg_sets[which]

        def apply_block(state_now, block_items):
            key_block, value_block, key_pos, key_seg = block_items
            needed = (key_pos[0] <= query_pos[-1]) & (key_seg[-1] >= query_seg[0])

            def compute(inner_state):
                return block_update(
                    inner_state,
                    query_block,
                    query_pos,
                    query_seg,
                    key_block,
                    value_block,
                    key_pos,
                    key_seg,
                    score_scale,
                )

            def keep_state(inner_state):
                return inner_state

            return (lax.cond(needed, compute, keep_state, state_now), None)

        new_state, _ = lax.scan(
            apply_block, carry_state[which], (key_blocks, value_blocks, key_positions, key_segments)
        )
        updated.append(new_state)
    folded = (updated[0], updated[1])
    outputs = []
    for softmax_state in folded:
        running_max, running_sum, accum = softmax_state
        normed = accum / jnp.transpose(running_sum, (2, 0, 1))[..., None]
        outputs.append(
            normed.reshape(half_rows, head_local * group_width * HEAD_WIDTH).astype(jnp.bfloat16)
        )
    first_out = outputs[0]
    second_out = outputs[1]
    attended = jnp.concatenate([first_out, second_out], axis=0)
    return lax.psum_scatter(
        jnp.dot(attended, out_weight, preferred_element_type=jnp.float32).astype(jnp.bfloat16),
        "kv",
        scatter_dimension=0,
        tiled=True,
    )


def solution(mesh):
    return jax.shard_map(
        on_device,
        mesh=mesh,
        in_specs=(P("ctx", "kv"), P("ctx", "kv"), P("ctx", "kv"), P(), P("kv", None)),
        out_specs=P(("ctx", "kv"), None),
        check_vma=False,
    )
```

profile of v0, /device:TPU:10, one launch (start us, length us, event | category | flops | bytes accessed | tf_op | source)
XLA Modules:
  0.0 1019.1 jit_solution(8191775920251826591)
XLA Ops:
  6.5 0.7 all-gather.3.cloned.1.call-update
  7.3 0.7 all-gather.5.cloned.1.call-update
  8.1 0.7 copy.26
  9.3 1.3 fusion.50
  11.7 160.4 %all-gather.3.cloned.1.call-done = bf16[16384,256]{1,0:T(8,128)(2,1)} async-done(((bf16[512,256]{1,0:T(8,128)(2,1)}), bf16[16384,256]{1,0:T(8,128)(2,1)}) %all-gather.3.cloned.1.call-update) | async-done | bytes 8388624 | tf_op jit(solution)/shard_map/all_gather | solution.py:75
  172.1 12.5 %reshape.98 = bf16[32,512,2,128]{3,2,1,0:T(2,128)(2,1)} reshape(bf16[16384,256]{1,0:T(8,128)(2,1)} %all-gather.3.cloned.1.call-done) | data formatting | bytes 16777216 | tf_op jit(solution)/shard_map/reshape | solution.py:80
  184.7 8.8 copy.30
  193.5 148.4 %all-gather.5.cloned.1.call-done = bf16[16384,256]{1,0:T(8,128)(2,1)} async-done(((bf16[512,256]{1,0:T(8,128)(2,1)}), bf16[16384,256]{1,0:T(8,128)(2,1)}) %all-gather.5.cloned.1.call-update) | async-done | bytes 8388624 | tf_op jit(solution)/shard_map/all_gather | solution.py:76
  341.9 12.5 %reshape.99 = bf16[32,512,2,128]{3,2,1,0:T(2,128)(2,1)} reshape(bf16[16384,256]{1,0:T(8,128)(2,1)} %all-gather.5.cloned.1.call-done) | data formatting | bytes 16777216 | tf_op jit(solution)/shard_map/reshape | solution.py:81
  354.4 8.8 copy.32
  363.3 180.4 %while.28 = (s32[]{:T(128)}, f32[2,4,256]{2,1,0:T(4,128)S(1)}, f32[2,4,256]{2,1,0:T(4,128)S(1)}, f32[256,2,4,128]{3,0,2,1:T(8,128)S(1)}, s32[32,512]{1,0:T(8,128...) while((s32[]{:T(128)}, f32[2,4,256]{2,1,0:T(4,128)S(1)}, ...), condition=%wide.region_8.9_spmd, body=%wide.region_3.8_spmd.sunk | while | flops 551426048 | bytes 16399719 | solution.py:113
  366.3 0.7 slice.42
  371.2 0.7 slice.42
  376.1 0.7 slice.42
  378.0 5.7 conditional.4
  378.3 1.7 fusion
  380.0 1.0 fusion.2
  381.1 2.7 fusion.9
  386.7 0.7 slice.42
  388.7 5.7 conditional.4
  388.9 1.7 fusion
  390.7 1.0 fusion.2
  391.7 2.7 fusion.9
  397.4 0.7 slice.42
  399.3 5.7 conditional.4
  399.5 1.7 fusion
  401.3 1.0 fusion.2
  402.3 2.7 fusion.9
  408.0 0.7 slice.42
  409.9 5.7 conditional.4
  410.1 1.7 fusion
  411.9 1.0 fusion.2
  412.9 2.7 fusion.9
  418.6 0.7 slice.42
  423.5 0.7 slice.42
  428.5 0.7 slice.42
  433.4 0.7 slice.42
  438.3 0.7 slice.42
  443.2 0.7 slice.42
  448.2 0.7 slice.42
  527.0 0.7 slice.42
  544.1 180.4 %while.29 = (s32[]{:T(128)}, f32[2,4,256]{2,1,0:T(4,128)S(1)}, f32[2,4,256]{2,1,0:T(4,128)S(1)}, f32[256,2,4,128]{3,0,2,1:T(8,128)S(1)}, s32[32,512]{1,0:T(8,128...) while((s32[]{:T(128)}, f32[2,4,256]{2,1,0:T(4,128)S(1)}, ...), condition=%wide.region_15.16_spmd, body=%wide.region_10.15_spmd.sunk | while | flops 551426048 | bytes 16399719 | solution.py:113
  558.9 5.7 conditional.5
  559.1 1.7 fusion.23
  560.8 1.0 fusion.25
  561.9 2.7 fusion.32
  567.6 0.7 slice.44
  569.5 5.7 conditional.5
  569.7 1.7 fusion.23
  571.5 1.0 fusion.25
  572.5 2.7 fusion.32
  580.1 5.7 conditional.5
  580.3 1.7 fusion.23
  582.1 1.0 fusion.25
  583.1 2.7 fusion.32
  590.7 5.7 conditional.5
  591.0 1.7 fusion.23
  592.7 1.0 fusion.25
  593.8 2.7 fusion.32
  643.8 0.7 slice.44
  724.5 1.3 copy.38
  725.9 1.3 divide_convert_fusion
  727.2 9.6 convolution_convert_fusion
  736.9 275.7 %reduce-scatter.2.cloned.1.call-done = bf16[128,4096]{1,0:T(8,128)(2,1)} async-done(((bf16[512,4096]{1,0:T(8,128)(2,1)}), bf16[128,4096]{1,0:T(8,128)(2,1)}) %reduce-scatter.2.cloned.1.call-update) | async-done | bytes 1048592 | tf_op jit(solution)/shard_map/reduce_scatter | solution.py:128
  (415 shorter events, 145.5 us)
Async XLA Ops:
  6.5 165.6 %all-gather.3.cloned.1.call-start = ((), (), s32[]{:S(2)}) async-start(), calls=%async_computation.1 | async-start | bytes 8650752 | tf_op jit(solution)/shard_map/all_gather | solution.py:75
  7.3 334.6 %all-gather.5.cloned.1.call-start = ((), (), s32[]{:S(2)}) async-start(), calls=%async_computation.2 | async-start | bytes 8650752 | tf_op jit(solution)/shard_map/all_gather | solution.py:76
  8.0 1004.6 %reduce-scatter.2.cloned.1.call-start = ((), (), s32[]{:S(2)}) async-start(), calls=%async_computation.3 | async-start | bytes 5242880 | tf_op jit(solution)/shard_map/reduce_scatter | solution.py:128
Sparse Core Ops, SparseCore 0:
  9.0 163.0 all-gather.2
  173.8 168.0 all-gather.4
  737.0 275.5 reduce-scatter.1
where the time goes:
time: 1030 us; the launch traced here: 1020 us
  waiting for transfers between devices  586 us (57%)
  local copies, waits for them, and re-layouts  199 us (19%)
  loops' own time  164 us (16%)
  matrix products  44.9 us (4%)
  between operations  13.2 us (1%)
  other arithmetic  12 us (1%)
    reduce_scatter x1, waiting for transfers between devices, on_device(): lax.psum_scatter(jnp.dot(attended, out_weight, preferred_element_type=jnp...  276 us
    another operation x2, loops' own time, on_device(): lax.scan(apply_block, carry_state[which], (key_blocks, value_blocks, key_...  163 us
    all_gather x1, waiting for transfers between devices, on_device(): key_piece = lax.all_gather(keys, 'ctx', axis=0, tiled=True)  160 us
    slice x256, local copies, waits for them, and re-layouts, apply_block(): needed = (key_pos[0] <= query_pos[-1]) & (key_seg[-1] >= query_seg[0])  150 us
    all_gather x1, waiting for transfers between devices, on_device(): value_piece = lax.all_gather(values, 'ctx', axis=0, tiled=True)  148 us
    dot_general x8, matrix products, block_update(): jnp.einsum('hgqk,khd->qhgd', rounded, value_block, preferred_element_type...  21.4 us
  transfers between devices with their start and end apart: 3, of which 3 were waited for; matrix products, arithmetic and copies ran while one was open for 2% of the time, Pallas kernels for 0%

commit v1 on v0

v1 whole, which is shorter than its diff:
```python
import functools
import math

import jax
import jax.numpy as jnp
from jax import lax
from jax.experimental import pallas as pl
from jax.experimental.pallas import tpu as pltpu
from jax.sharding import PartitionSpec as P

HEAD_WIDTH = 128
NEG = -1e30
AXES = ("ctx", "kv")
SCALE2 = HEAD_WIDTH ** -0.5 * math.log2(math.e)
HALF = 256


def device_at(z, y_hi, y_lo, x, c):
    return ((z % 4) * 8 + y_lo * 4 + x % 4) * 4 + y_hi * 2 + c


def permutation(move):
    pairs = []
    for i in range(128):
        ctx, kv = divmod(i, 4)
        pairs.append((i, device_at(*move(ctx // 8, kv // 2, ctx // 4 % 2, ctx % 4, kv % 2))))
    return pairs


X_UP = permutation(lambda z, yh, yl, x, c: (z, yh, yl, x + 1, c))
X_DOWN = permutation(lambda z, yh, yl, x, c: (z, yh, yl, x + 3, c))
Y_LO = permutation(lambda z, yh, yl, x, c: (z, yh, 1 - yl, x, c))
Y_HI = permutation(lambda z, yh, yl, x, c: (z, 1 - yh, yl, x, c))
CORE = permutation(lambda z, yh, yl, x, c: (z, yh, yl, x, 1 - c))
TO_HEAD = [
    permutation(lambda z, yh, yl, x, c, k=k: (2 * c + (z ^ k) // 2, yh, yl, x, (z ^ k) % 2))
    for k in range(4)
]
TO_HOME = [[(b, a) for a, b in pairs] for pairs in TO_HEAD]


def send(x, pairs):
    return lax.ppermute(x, AXES, pairs)


def dot_nt(a, b):
    return lax.dot_general(a, b, (((1,), (1,)), ((), ())), preferred_element_type=jnp.float32)


def attention_kernel(first, last, info_ref, ends_ref, lo_ref, hi_ref, q_ref, mine_ref, other_ref, *refs):
    if first:
        acc_in = m_in = l_in = None
    else:
        acc_in, m_in, l_in = refs[:3]
        refs = refs[3:]
    if last:
        out_ref, acc, m_s, l_s, start_s = refs
    else:
        acc_out, m_out, l_out, acc, m_s, l_s, start_s = refs
    own_j = info_ref[4]
    core = info_ref[5]

    def q_block(qb, carry):
        zq = qb // 2
        hq = qb % 2
        gq = (zq * 8 + own_j) * 2 + hq
        rows = pl.ds(pl.multiple_of(qb * HALF, HALF), HALF)
        q_pos = gq * HALF + lax.broadcasted_iota(jnp.int32, (HALF, 128), 0)
        start = jnp.zeros((HALF, 128), jnp.int32)
        for doc in range(16):
            end = ends_ref[doc]
            start = jnp.maximum(start, jnp.where(q_pos >= end, end, 0))
        start_s[...] = start
        if first:
            acc[...] = jnp.zeros_like(acc)
            m_s[...] = jnp.full_like(m_s, NEG)
            l_s[...] = jnp.zeros_like(l_s)
        else:
            acc[...] = acc_in[rows, :]
            m_s[...] = m_in[rows, :]
            l_s[...] = l_in[rows, :]
        lo = lo_ref[gq]
        hi = hi_ref[gq]

        def update(slot, zk, gk, masked):
            k_all = jnp.concatenate([mine_ref[slot, zk, :, :128], other_ref[slot, zk, :, :128]], axis=0)
            v_all = jnp.concatenate([mine_ref[slot, zk, :, 128:], other_ref[slot, zk, :, 128:]], axis=0)
            if masked:
                column = lax.broadcasted_iota(jnp.int32, (HALF, 2 * HALF), 1)
                k_pos = gk * (2 * HALF) + jnp.where(core == 0, column, column ^ HALF)
                q_at = gq * HALF + lax.broadcasted_iota(jnp.int32, (HALF, 2 * HALF), 0)
                allowed = (k_pos <= q_at) & (k_pos >= start_s[:, :1])
            for h in range(2):
                cols = slice(h * 128, (h + 1) * 128)
                s = dot_nt(q_ref[rows, cols], k_all)
                if masked:
                    s = jnp.where(allowed, s, NEG)
                m_old = m_s[:, cols]
                m_new = jnp.maximum(m_old, jnp.max(s, axis=1, keepdims=True))
                shrink = jnp.exp2((m_old - m_new) * SCALE2)
                p = jnp.exp2((s - m_new[:, :1]) * SCALE2)
                if masked:
                    p = jnp.where(allowed, p, 0.0)
                m_s[:, cols] = m_new
                l_s[:, cols] = l_s[:, cols] * shrink + jnp.sum(p, axis=1, keepdims=True)
                acc[:, cols] = acc[:, cols] * shrink + jnp.dot(
                    p.astype(jnp.bfloat16), v_all, preferred_element_type=jnp.float32
                )

        def k_block(kb, carry):
            slot = kb // 4
            zk = kb % 4
            gk = zk * 8 + info_ref[slot]
            needed = (gk * 512 <= gq * HALF + HALF - 1) & (gk * 512 + 511 >= lo)
            full = (gk * 512 + 511 <= gq * HALF) & (gk * 512 >= hi)

            @pl.when(full)
            def _():
                update(slot, zk, gk, False)

            @pl.when(needed & jnp.logical_not(full))
            def _():
                update(slot, zk, gk, True)

            return carry

        lax.fori_loop(0, 16, k_block, 0)
        if last:
            out_ref[rows, :] = (acc[...] / l_s[...]).astype(jnp.bfloat16)
        else:
            acc_out[rows, :] = acc[...]
            m_out[rows, :] = m_s[...]
            l_out[rows, :] = l_s[...]
        return carry

    lax.fori_loop(0, 8, q_block, 0)


def attention(first, last, info, ends, lo, hi, q, mine, other, state):
    rows = q.shape[0]
    whole = pl.BlockSpec(memory_space=pltpu.VMEM)
    scalar = pl.BlockSpec(memory_space=pltpu.SMEM)
    wide = jax.ShapeDtypeStruct((rows, 256), jnp.float32)
    return pl.pallas_call(
        functools.partial(attention_kernel, first, last),
        out_shape=jax.ShapeDtypeStruct((rows, 256), jnp.bfloat16) if last else (wide, wide, wide),
        in_specs=[scalar] * 4 + [whole] * (3 if first else 6),
        out_specs=whole if last else (whole, whole, whole),
        scratch_shapes=[pltpu.VMEM((HALF, 256), jnp.float32)] * 3 + [pltpu.VMEM((HALF, 128), jnp.int32)],
        compiler_params=pltpu.CompilerParams(vmem_limit_bytes=50 * 1024 * 1024),
        cost_estimate=pl.CostEstimate(
            flops=12_000_000_000, bytes_accessed=8 * 1024 * 1024, transcendentals=12_000_000
        ),
        name="attend_last" if last else "attend_first",
    )(info, ends, lo, hi, q, mine, other, *state)


def pick(stacked, index):
    return lax.dynamic_index_in_dim(stacked, index, 0, keepdims=False)


def on_device(queries, keys, values, doc_lengths, out_weight):
    ctx = lax.axis_index("ctx")
    kv = lax.axis_index("kv")
    z, y_lo, x = ctx // 8, ctx // 4 % 2, ctx % 4
    y_hi, core = kv // 2, kv % 2
    j = ctx % 8
    mine_d = 2 * (z % 2) + core
    ends = jnp.cumsum(doc_lengths).astype(jnp.int32)
    blocks = jnp.arange(64, dtype=jnp.int32) * HALF

    def start_of(position):
        return jnp.max(jnp.where(ends[None, :] <= position[:, None], ends[None, :], 0), axis=1)

    lo, hi = start_of(blocks), start_of(blocks + HALF - 1)

    halves_k = keys.reshape(2, HALF, 2, 128)
    halves_v = values.reshape(2, HALF, 2, 128)
    packed = jnp.concatenate([halves_k, halves_v], axis=3)
    pieces = jnp.transpose(packed, (2, 0, 1, 3)).reshape(4, HALF, 256)
    got = jnp.stack([send(pick(pieces, z ^ k), TO_HEAD[k]) for k in range(4)])
    a0 = jnp.stack([pick(got, mine_d ^ plane) for plane in range(4)])

    q_pieces = jnp.transpose(queries.reshape(512, 4, 256), (1, 0, 2))
    q_got = jnp.stack([send(pick(q_pieces, z ^ k), TO_HEAD[k]) for k in range(4)])
    q = jnp.concatenate([pick(q_got, mine_d ^ plane) for plane in range(4)], axis=0)

    a1 = send(a0, X_DOWN)
    a3 = send(a0, X_UP)
    b0 = send(a0, Y_LO)
    near = jnp.stack([a0, a1, a3, b0])
    near_other = send(near, CORE)
    b1 = send(b0, X_DOWN)
    b3 = send(b0, X_UP)
    low = send(jnp.concatenate([a1[:2], b1[:2]], axis=0), X_DOWN)
    high = send(jnp.concatenate([a3[2:], b3[2:]], axis=0), X_UP)
    far = jnp.stack(
        [b1, b3, jnp.concatenate([low[:2], high[:2]], axis=0), jnp.concatenate([low[2:], high[2:]], axis=0)]
    )
    far_other = send(far, CORE)

    here, there = y_lo * 4, (1 - y_lo) * 4
    near_info = jnp.stack([here + x, here + (x + 1) % 4, here + (x + 3) % 4, there + x, j, core]).astype(jnp.int32)
    far_info = jnp.stack(
        [there + (x + 1) % 4, there + (x + 3) % 4, here + (x + 2) % 4, there + (x + 2) % 4, j, core]
    ).astype(jnp.int32)
    state = attention(True, False, near_info, ends, lo, hi, q, near, near_other, ())
    out = attention(False, True, far_info, ends, lo, hi, q, far, far_other, state)

    planes = out.reshape(4, 512, 256)
    back = jnp.stack([send(pick(planes, mine_d ^ k), TO_HOME[k]) for k in range(4)])
    attended = jnp.concatenate([pick(back, z ^ d) for d in range(4)], axis=1)

    by_half = attended.reshape(2, 256, 1024)

    def project(which):
        part = jnp.dot(pick(by_half, which), out_weight, preferred_element_type=jnp.float32).astype(jnp.bfloat16)
        part = part.reshape(2, 128, 4096)
        arrived = send(pick(part, 1 - core), CORE)
        return pick(part, core).astype(jnp.float32) + arrived.astype(jnp.float32)

    far_sum = send(project(1 - y_hi).astype(jnp.bfloat16), Y_HI)
    return (project(y_hi) + far_sum.astype(jnp.float32)).astype(jnp.bfloat16)


def solution(mesh):
    return jax.shard_map(
        on_device,
        mesh=mesh,
        in_specs=(P("ctx", "kv"), P("ctx", "kv"), P("ctx", "kv"), P(), P("kv", None)),
        out_specs=P(("ctx", "kv"), None),
        check_vma=False,
    )
```

time: 1030 us -> 271 us (0.26); the launches traced: 1020 us -> 274 us
  waiting for transfers between devices: 586 us -> 83.6 us
  local copies, waits for them, and re-layouts: 199 us -> 11.2 us
  loops' own time: 164 us -> 0 us
  Pallas kernels: 0 us -> 130 us
  matrix products: 44.9 us -> 8.21 us
  starting transfers between devices: 0.08 us -> 33 us
  between operations: 13.2 us -> 0.69 us
    all_gather x2 -> x0, waiting for transfers between devices: 309 us -> none  [the longest x1 160 us: on_device(): key_piece = lax.all_gather(keys, 'ctx', axis=0, tiled=True)]
    reduce_scatter x1 -> x0, waiting for transfers between devices: 276 us -> none  [on_device(): lax.psum_scatter(jnp.dot(attended, out_weight, preferred_element_type=jnp...]
    another operation x66 -> x0, loops' own time: 164 us -> none  [the longest x2 163 us: on_device(): lax.scan(apply_block, carry_state[which], (key_blocks, value_blocks, key_...]
    slice x257 -> x6, local copies, waits for them, and re-layouts: 152 us -> 2.27 us  [the longest x1 1.13 us: on_device(): low[:2]]
    pallas_call x0 -> x2, Pallas kernels: none -> 130 us  [attention(): pl.pallas_call(functools.partial(attention_kernel, first, last), out_shap...]
    ppermute x0 -> x24, waiting for transfers between devices: none -> 83.6 us  [send(): return lax.ppermute(x, AXES, pairs)]
    dot_general x17 -> x2, matrix products: 44.9 us -> 8.21 us  [project(): jnp.dot(pick(by_half, which), out_weight, preferred_element_type=jnp.floa...]
    ppermute x0 -> x24, starting transfers between devices: none -> 33 us  [send(): return lax.ppermute(x, AXES, pairs)]
  transfers between devices with their start and end apart: 3 -> 24, of which waited for: 3 -> 13; matrix products, arithmetic and copies ran while one was open for 2% -> 5% of each run, Pallas kernels for 0% -> 26%
where the time goes in v1:
time: 271 us; the launch traced here: 274 us
  Pallas kernels  130 us (48%)
  waiting for transfers between devices  83.6 us (31%)
  starting transfers between devices  33 us (12%)
  local copies, waits for them, and re-layouts  11.2 us (4%)
  matrix products  8.21 us (3%)
  other arithmetic  8.01 us (3%)
    pallas_call x2, Pallas kernels, attention(): pl.pallas_call(functools.partial(attention_kernel, first, last), out_shap...  130 us
    ppermute x24, waiting for transfers between devices, send(): return lax.ppermute(x, AXES, pairs)  83.6 us
    ppermute x24, starting transfers between devices, send(): return lax.ppermute(x, AXES, pairs)  33 us
    dot_general x2, matrix products, project(): jnp.dot(pick(by_half, which), out_weight, preferred_element_type=jnp.floa...  8.21 us
  transfers between devices with their start and end apart: 24, of which 13 were waited for; matrix products, arithmetic and copies ran while one was open for 5% of the time, Pallas kernels for 26%

profile of v1, /device:TPU:10, one launch (start us, length us, event | category | flops | bytes accessed | tf_op | source)
XLA Modules:
  0.0 274.3 jit_solution(2949553077296063432)
XLA Ops:
  0.0 1.0 reshape.75
  1.0 1.0 reshape.76
  2.0 0.6 maximum_bitcast_fusion
  2.8 0.7 collective-permute-start.4
  3.4 5.3 %collective-permute-start.5 = (bf16[256,256]{1,0:T(8,128)(2,1)S(1)}, bf16[256,256]{1,0:T(8,128)(2,1)S(1)}, u32[]{:S(2)}, u32[]{:S(2)}) collective-permute-start(bf16[256,256]{1,0:T(8,128)(2,1)S(1)} %get-tuple-element.42), channel_id=1, source_target_pairs={{0,1},{1,65},{2,3},{3,67},{4,5},{5,69},{6,7},{7,71},{8,9},{9,73},{... | collective-permute-start | bytes 393224 | tf_op jit(solution)/shard_map/ppermute | solution.py:43
  8.8 2.6 collective-permute-start.7
  11.5 3.9 %collective-permute-done.6 = bf16[256,256]{1,0:T(8,128)(2,1)S(1)} collective-permute-done((bf16[256,256]{1,0:T(8,128)(2,1)S(1)}, bf16[256,256]{1,0:T(8,128)(2,1)S(1)}, u32[]{:S(2)}, u32[]{:S(2)}) %collective-permute-start.6) | collective-permute-done | bytes 131104 | tf_op jit(solution)/shard_map/ppermute | solution.py:43
  15.4 4.1 %collective-permute-done.7 = bf16[256,256]{1,0:T(8,128)(2,1)S(1)} collective-permute-done((bf16[256,256]{1,0:T(8,128)(2,1)S(1)}, bf16[256,256]{1,0:T(8,128)(2,1)S(1)}, u32[]{:S(2)}, u32[]{:S(2)}) %collective-permute-start.7) | collective-permute-done | bytes 131104 | tf_op jit(solution)/shard_map/ppermute | solution.py:43
  19.7 0.1 fusion.9
  19.8 0.5 collective-permute-start.8
  20.3 0.5 collective-permute-start.11
  20.8 11.3 %collective-permute-done.8 = bf16[4,256,256]{2,1,0:T(8,128)(2,1)S(1)} collective-permute-done((bf16[4,256,256]{2,1,0:T(8,128)(2,1)S(1)}, bf16[4,256,256]{2,1,0:T(8,128)(2,1)S(1)}, u32[]{:S(2)}, u32[]{:S(2)}) %collective-permute-start.8) | collective-permute-done | bytes 524320 | tf_op jit(solution)/shard_map/ppermute | solution.py:43
  32.1 0.5 collective-permute-start.9
  32.6 1.5 collective-permute-start.13
  34.1 1.5 collective-permute-start.10
  35.7 7.9 %collective-permute-done.9 = bf16[4,256,256]{2,1,0:T(8,128)(2,1)S(1)} collective-permute-done((bf16[4,256,256]{2,1,0:T(8,128)(2,1)S(1)}, bf16[4,256,256]{2,1,0:T(8,128)(2,1)S(1)}, u32[]{:S(2)}, u32[]{:S(2)}) %collective-permute-start.9) | collective-permute-done | bytes 524320 | tf_op jit(solution)/shard_map/ppermute | solution.py:43
  43.5 0.8 copy-done.2
  44.3 0.9 pad_maximum_fusion.8
  45.2 0.8 collective-permute-start.12
  46.0 2.2 collective-permute-done.13
  48.2 0.3 pad_maximum_fusion.1.mine_ref
  48.5 0.1 collective-permute-start.16
  48.6 7.3 %collective-permute-done.10 = bf16[4,256,256]{2,1,0:T(8,128)(2,1)S(1)} collective-permute-done((bf16[4,256,256]{2,1,0:T(8,128)(2,1)S(1)}, bf16[4,256,256]{2,1,0:T(8,128)(2,1)S(1)}, u32[]{:S(2)}, u32[]{:S(2)}) %collective-permute-start.10) | collective-permute-done | bytes 524320 | tf_op jit(solution)/shard_map/ppermute | solution.py:43
  56.0 0.9 pad_maximum_fusion.9
  56.9 0.5 collective-permute-start.14
  57.4 1.5 copy.18
  58.9 0.9 constant_dynamic-slice_fusion.11
  59.8 1.1 copy.20
  61.0 1.1 fusion.10
  62.1 6.4 %collective-permute-done.14 = bf16[4,256,256]{2,1,0:T(8,128)(2,1)} collective-permute-done((bf16[4,256,256]{2,1,0:T(8,128)(2,1)}, bf16[4,256,256]{2,1,0:T(8,128)(2,1)}, u32[]{:S(2)}, u32[]{:S(2)}) %collective-permute-start.14) | collective-permute-done | bytes 524320 | tf_op jit(solution)/shard_map/ppermute | solution.py:43
  68.6 1.1 fusion.11
  69.6 0.1 maximum_bitcast_fusion.1
  69.8 1.6 pad_maximum_fusion.mine_ref
  71.4 0.1 copy.21
  71.6 4.3 %collective-permute-start.2 = (bf16[512,256]{1,0:T(8,128)(2,1)S(1)}, bf16[512,256]{1,0:T(8,128)(2,1)}, u32[]{:S(2)}, u32[]{:S(2)}) collective-permute-start(bf16[512,256]{1,0:T(8,128)(2,1)S(1)} %bitcast.107), channel_id=1, source_target_pairs={{0,32},{1,96},{2,34},{3,98},{4,36},{5,100},{6,38},{7,102},{8,40},{... | collective-permute-start | bytes 786440 | tf_op jit(solution)/shard_map/ppermute | solution.py:43
  75.9 0.1 copy.22
  76.0 2.0 collective-permute-start.3
  78.1 0.1 copy.19
  78.2 0.9 collective-permute-start
  79.3 0.1 reduce.ends_ref
  79.4 0.1 stack.147.info_ref
  79.6 0.1 select_reduce_fusion
  79.8 8.1 %collective-permute-done.3 = bf16[512,256]{1,0:T(8,128)(2,1)} collective-permute-done((bf16[512,256]{1,0:T(8,128)(2,1)S(1)}, bf16[512,256]{1,0:T(8,128)(2,1)}, u32[]{:S(2)}, u32[]{:S(2)}) %collective-permute-start.3) | collective-permute-done | bytes 262176 | tf_op jit(solution)/shard_map/ppermute | solution.py:43
  87.9 1.2 pad_maximum_fusion.2
  89.3 70.6 %attend_first.1 = (f32[2048,256]{1,0:T(8,128)S(1)}, f32[2048,256]{1,0:T(8,128)}, f32[2048,256]{1,0:T(8,128)}) custom-call(s32[6]{0:T(128)S(1)} %stack.147.info_ref, s32[16]{0:T(128)S(1)} %reduce.ends_ref, s32[64]{0:T(128)S(1)} %get-tuple-element.12.lo_ref, s32[64]{0:T(128)S(1)} %get-tuple-element.11.hi_ref, bf16[2048,256]{1,0:T(8,128)(2,1)S(1)} %pad_maximum_fusion.3.q_ref, ...), custom_call_target="tpu_custom_call" | custom-call | flops 12000000000 | bytes 8388608 | tf_op jit(solution)/shard_map/attend_first/pallas_call | solution.py:144
  159.9 1.4 copy-done
  161.2 59.0 %attend_last.1 = bf16[2048,256]{1,0:T(8,128)(2,1)S(1)} custom-call(s32[6]{0:T(128)S(1)} %stack.126.info_ref, s32[16]{0:T(128)S(1)} %reduce.ends_ref, s32[64]{0:T(128)S(1)} %get-tuple-element.12.lo_ref, s32[64]{0:T(128)S(1)} %get-tuple-element.11.hi_ref, bf16[2048,256]{1,0:T(8,128)(2,1)S(1)} %pad_maximum_fusion.3.q_ref, ...), custom_call_target="tpu_custom_call" | custom-call | flops 12000000000 | bytes 8388608 | tf_op jit(solution)/shard_map/attend_last/pallas_call | solution.py:144
  220.4 0.7 collective-permute-start.17
  221.1 2.7 collective-permute-start.18
  223.8 2.3 collective-permute-start.19
  226.1 2.4 collective-permute-start.20
  228.6 1.2 collective-permute-done.18
  229.8 6.5 %collective-permute-done.19 = bf16[512,256]{1,0:T(8,128)(2,1)S(1)} collective-permute-done((bf16[512,256]{1,0:T(8,128)(2,1)S(1)}, bf16[512,256]{1,0:T(8,128)(2,1)S(1)}, u32[]{:S(2)}, u32[]{:S(2)}) %collective-permute-start.19) | collective-permute-done | bytes 262176 | tf_op jit(solution)/shard_map/ppermute | solution.py:43
  236.3 0.2 collective-permute-done.20
  236.5 0.1 pad_maximum_fusion.4
  236.7 0.1 pad_maximum_fusion.5
  236.9 5.9 %convolution_convert_fusion = bf16[256,4096]{1,0:T(8,128)(2,1)S(1)} fusion(bf16[1024,4096]{1,0:T(8,128)(2,1)} %param.9, bf16[2,256,1024]{2,1,0:T(8,128)(2,1)S(1)} %pad_maximum_fusion.5, s32[]{:T(128)S(6)} %select_n.140), kind=kOutput, calls=%fused_computation | convolution fusion | flops 2148532224 | bytes 11010052 | tf_op jit(solution)/shard_map/dot_general | solution.py:217
  242.7 0.1 dynamic-slice_bitcast_fusion
  243.0 2.3 convolution_convert_fusion.1
  245.4 0.6 collective-permute-start.21
  246.0 0.2 fusion
  246.2 2.4 collective-permute-start.23
  248.6 24.3 %collective-permute-done.23 = bf16[128,4096]{1,0:T(8,128)(2,1)S(1)} collective-permute-done((bf16[128,4096]{1,0:T(8,128)(2,1)S(1)}, bf16[128,4096]{1,0:T(8,128)(2,1)S(1)}, u32[]{:S(2)}, u32[]{:S(2)}) %collective-permute-start.23) | collective-permute-done | bytes 1048608 | tf_op jit(solution)/shard_map/ppermute | solution.py:43
  272.9 1.4 fusion.2
  (54 shorter events, 1.2 us)
Async XLA Ops:
  2.8 8.7 %collective-permute-start.4 = (bf16[256,256]{1,0:T(8,128)(2,1)S(1)}, bf16[256,256]{1,0:T(8,128)(2,1)S(1)}, u32[]{:S(2)}, u32[]{:S(2)}) collective-permute-start(bf16[256,256]{1,0:T(8,128)(2,1)S(1)} %get-tuple-element.39), channel_id=1, source_target_pairs={{0,0},{1,64},{2,2},{3,66},{4,4},{5,68},{6,6},{7,70},{8,8},{9,72},{... | collective-permute-start | bytes 393224 | tf_op jit(solution)/shard_map/ppermute | solution.py:43
  3.4 8.0 %collective-permute-start.5 = (bf16[256,256]{1,0:T(8,128)(2,1)S(1)}, bf16[256,256]{1,0:T(8,128)(2,1)S(1)}, u32[]{:S(2)}, u32[]{:S(2)}) collective-permute-start(bf16[256,256]{1,0:T(8,128)(2,1)S(1)} %get-tuple-element.42), channel_id=1, source_target_pairs={{0,1},{1,65},{2,3},{3,67},{4,5},{5,69},{6,7},{7,71},{8,9},{9,73},{... | collective-permute-start | bytes 393224 | tf_op jit(solution)/shard_map/ppermute | solution.py:43
  8.8 6.7 %collective-permute-start.6 = (bf16[256,256]{1,0:T(8,128)(2,1)S(1)}, bf16[256,256]{1,0:T(8,128)(2,1)S(1)}, u32[]{:S(2)}, u32[]{:S(2)}) collective-permute-start(bf16[256,256]{1,0:T(8,128)(2,1)S(1)} %get-tuple-element.41), channel_id=1, source_target_pairs={{0,32},{1,96},{2,34},{3,98},{4,36},{5,100},{6,38},{7,102},{8,40},{... | collective-permute-start | bytes 393224 | tf_op jit(solution)/shard_map/ppermute | solution.py:43
  8.8 10.8 %collective-permute-start.7 = (bf16[256,256]{1,0:T(8,128)(2,1)S(1)}, bf16[256,256]{1,0:T(8,128)(2,1)S(1)}, u32[]{:S(2)}, u32[]{:S(2)}) collective-permute-start(bf16[256,256]{1,0:T(8,128)(2,1)S(1)} %get-tuple-element.40), channel_id=1, source_target_pairs={{0,33},{1,97},{2,35},{3,99},{4,37},{5,101},{6,39},{7,103},{8,41},{... | collective-permute-start | bytes 393224 | tf_op jit(solution)/shard_map/ppermute | solution.py:43
  19.8 12.3 %collective-permute-start.8 = (bf16[4,256,256]{2,1,0:T(8,128)(2,1)S(1)}, bf16[4,256,256]{2,1,0:T(8,128)(2,1)S(1)}, u32[]{:S(2)}, u32[]{:S(2)}) collective-permute-start(bf16[4,256,256]{2,1,0:T(8,128)(2,1)S(1)} %get-tuple-element.30), channel_id=1, source_target_pairs={{0,16},{1,17},{2,18},{3,19},{4,20},{5,21},{6,22},{7,23},{8,24},{9,... | collective-permute-start | bytes 1572872 | tf_op jit(solution)/shard_map/ppermute | solution.py:43
  20.3 15.3 %collective-permute-start.11 = (bf16[4,256,256]{2,1,0:T(8,128)(2,1)S(1)}, bf16[4,256,256]{2,1,0:T(8,128)(2,1)S(1)}, u32[]{:S(2)}, u32[]{:S(2)}) collective-permute-start(bf16[4,256,256]{2,1,0:T(8,128)(2,1)S(1)} %get-tuple-element.30), channel_id=1, source_target_pairs={{0,12},{1,13},{2,14},{3,15},{4,0},{5,1},{6,2},{7,3},{8,4},{9,5},{1... | collective-permute-start | bytes 1572872 | tf_op jit(solution)/shard_map/ppermute | solution.py:43
  32.1 11.4 %collective-permute-start.9 = (bf16[4,256,256]{2,1,0:T(8,128)(2,1)S(1)}, bf16[4,256,256]{2,1,0:T(8,128)(2,1)S(1)}, u32[]{:S(2)}, u32[]{:S(2)}) collective-permute-start(bf16[4,256,256]{2,1,0:T(8,128)(2,1)S(1)} %collective-permute-done.8), channel_id=1, source_target_pairs={{0,12},{1,13},{2,14},{3,15},{4,0},{5,1},{6,2},{7,3},{8,4},{9,5},{1... | collective-permute-start | bytes 1572872 | tf_op jit(solution)/shard_map/ppermute | solution.py:43
  32.6 15.6 %collective-permute-start.13 = (bf16[4,256,256]{2,1,0:T(8,128)(2,1)S(1)}, bf16[4,256,256]{2,1,0:T(8,128)(2,1)S(1)}, u32[]{:S(2)}, u32[]{:S(2)}) collective-permute-start(bf16[4,256,256]{2,1,0:T(8,128)(2,1)S(1)} %get-tuple-element.30), channel_id=1, source_target_pairs={{0,4},{1,5},{2,6},{3,7},{4,8},{5,9},{6,10},{7,11},{8,12},{9,13},{1... | collective-permute-start | bytes 1572872 | tf_op jit(solution)/shard_map/ppermute | solution.py:43
  34.1 21.8 %collective-permute-start.10 = (bf16[4,256,256]{2,1,0:T(8,128)(2,1)S(1)}, bf16[4,256,256]{2,1,0:T(8,128)(2,1)S(1)}, u32[]{:S(2)}, u32[]{:S(2)}) collective-permute-start(bf16[4,256,256]{2,1,0:T(8,128)(2,1)S(1)} %collective-permute-done.8), channel_id=1, source_target_pairs={{0,4},{1,5},{2,6},{3,7},{4,8},{5,9},{6,10},{7,11},{8,12},{9,13},{1... | collective-permute-start | bytes 1572872 | tf_op jit(solution)/shard_map/ppermute | solution.py:43
  43.5 0.8 copy-start.2
  45.2 15.8 %collective-permute-start.12 = (bf16[4,256,256]{2,1,0:T(8,128)(2,1)}, bf16[4,256,256]{2,1,0:T(8,128)(2,1)}, u32[]{:S(2)}, u32[]{:S(2)}) collective-permute-start(bf16[4,256,256]{2,1,0:T(8,128)(2,1)} %pad_maximum_fusion.8), channel_id=1, source_target_pairs={{0,12},{1,13},{2,14},{3,15},{4,0},{5,1},{6,2},{7,3},{8,4},{9,5},{1... | collective-permute-start | bytes 1572872 | tf_op jit(solution)/shard_map/ppermute | solution.py:43
  48.5 10.4 %copy-start.1 = (bf16[4,4,256,256]{3,2,1,0:T(8,128)(2,1)}, bf16[4,4,256,256]{3,2,1,0:T(8,128)(2,1)S(1)}, u32[]{:S(2)}) copy-start(bf16[4,4,256,256]{3,2,1,0:T(8,128)(2,1)S(1)} %pad_maximum_fusion.1.mine_ref) | copy-start | bytes 6291460
  48.5 40.8 %collective-permute-start.16 = (bf16[4,4,256,256]{3,2,1,0:T(8,128)(2,1)S(1)}, bf16[4,4,256,256]{3,2,1,0:T(8,128)(2,1)}, u32[]{:S(2)}, u32[]{:S(2)}) collective-permute-start(bf16[4,4,256,256]{3,2,1,0:T(8,128)(2,1)S(1)} %pad_maximum_fusion.1.mine_ref), channel_id=1, source_target_pairs={{0,1},{1,0},{2,3},{3,2},{4,5},{5,4},{6,7},{7,6},{8,9},{9,8},{10,11... | collective-permute-start | bytes 6291464 | tf_op jit(solution)/shard_map/ppermute | solution.py:43
  55.9 1.0 copy-start.4
  56.9 11.7 %collective-permute-start.14 = (bf16[4,256,256]{2,1,0:T(8,128)(2,1)}, bf16[4,256,256]{2,1,0:T(8,128)(2,1)}, u32[]{:S(2)}, u32[]{:S(2)}) collective-permute-start(bf16[4,256,256]{2,1,0:T(8,128)(2,1)} %pad_maximum_fusion.9), channel_id=1, source_target_pairs={{0,4},{1,5},{2,6},{3,7},{4,8},{5,9},{6,10},{7,11},{8,12},{9,13},{1... | collective-permute-start | bytes 1572872 | tf_op jit(solution)/shard_map/ppermute | solution.py:43
  60.9 8.9 %copy-start.3 = (bf16[4,256,256]{2,1,0:T(8,128)(2,1)S(1)}, bf16[4,256,256]{2,1,0:T(8,128)(2,1)}, u32[]{:S(2)}) copy-start(bf16[4,256,256]{2,1,0:T(8,128)(2,1)} %copy-done.2) | copy-start | bytes 1572868
  60.9 8.9 %copy-start.5 = (bf16[4,256,256]{2,1,0:T(8,128)(2,1)S(1)}, bf16[4,256,256]{2,1,0:T(8,128)(2,1)}, u32[]{:S(2)}) copy-start(bf16[4,256,256]{2,1,0:T(8,128)(2,1)} %copy-done.4) | copy-start | bytes 1572868
  60.9 17.3 %collective-permute-start.1 = (bf16[512,256]{1,0:T(8,128)(2,1)S(1)}, bf16[512,256]{1,0:T(8,128)(2,1)}, u32[]{:S(2)}, u32[]{:S(2)}) collective-permute-start(bf16[512,256]{1,0:T(8,128)(2,1)S(1)} %bitcast.110), channel_id=1, source_target_pairs={{0,1},{1,65},{2,3},{3,67},{4,5},{5,69},{6,7},{7,71},{8,9},{9,73},{... | collective-permute-start | bytes 786440 | tf_op jit(solution)/shard_map/ppermute | solution.py:43
  69.8 1.7 copy-start.7
  69.8 6.1 %copy-start.6 = (bf16[512,1,256]{0,2,1:T(8,128)(2,1)S(1)}, bf16[512,1,256]{0,2,1:T(8,128)(2,1)}, u32[]{:S(2)}) copy-start(bf16[512,1,256]{0,2,1:T(8,128)(2,1)} %get-tuple-element.26) | copy-start | bytes 786436
  69.8 9.4 %copy-start.8 = (s32[16]{0:T(128)S(1)}, s32[16]{0:T(128)}, u32[]{:S(2)}) copy-start(s32[16]{0:T(128)} %param.8) | copy-start | bytes 196
  71.4 89.8 %collective-permute-start.15 = (bf16[4,4,256,256]{3,2,1,0:T(8,128)(2,1)}, bf16[4,4,256,256]{3,2,1,0:T(8,128)(2,1)}, u32[]{:S(2)}, u32[]{:S(2)}) collective-permute-start(bf16[4,4,256,256]{3,2,1,0:T(8,128)(2,1)} %pad_maximum_fusion.mine_ref), channel_id=1, source_target_pairs={{0,1},{1,0},{2,3},{3,2},{4,5},{5,4},{6,7},{7,6},{8,9},{9,8},{10,11... | collective-permute-start | bytes 6291464 | tf_op jit(solution)/shard_map/ppermute | solution.py:43
  71.6 8.2 %collective-permute-start.2 = (bf16[512,256]{1,0:T(8,128)(2,1)S(1)}, bf16[512,256]{1,0:T(8,128)(2,1)}, u32[]{:S(2)}, u32[]{:S(2)}) collective-permute-start(bf16[512,256]{1,0:T(8,128)(2,1)S(1)} %bitcast.107), channel_id=1, source_target_pairs={{0,32},{1,96},{2,34},{3,98},{4,36},{5,100},{6,38},{7,102},{8,40},{... | collective-permute-start | bytes 786440 | tf_op jit(solution)/shard_map/ppermute | solution.py:43
  76.0 11.9 %collective-permute-start.3 = (bf16[512,256]{1,0:T(8,128)(2,1)S(1)}, bf16[512,256]{1,0:T(8,128)(2,1)}, u32[]{:S(2)}, u32[]{:S(2)}) collective-permute-start(bf16[512,256]{1,0:T(8,128)(2,1)S(1)} %bitcast.108), channel_id=1, source_target_pairs={{0,33},{1,97},{2,35},{3,99},{4,37},{5,101},{6,39},{7,103},{8,41},{... | collective-permute-start | bytes 786440 | tf_op jit(solution)/shard_map/ppermute | solution.py:43
  78.2 9.7 %collective-permute-start = (bf16[512,256]{1,0:T(8,128)(2,1)S(1)}, bf16[512,256]{1,0:T(8,128)(2,1)S(1)}, u32[]{:S(2)}, u32[]{:S(2)}) collective-permute-start(bf16[512,256]{1,0:T(8,128)(2,1)S(1)} %bitcast.109), channel_id=1, source_target_pairs={{0,0},{1,64},{2,2},{3,66},{4,4},{5,68},{6,6},{7,70},{8,8},{9,72},{... | collective-permute-start | bytes 786440 | tf_op jit(solution)/shard_map/ppermute | solution.py:43
  159.9 1.4 copy-start
  220.4 8.2 %collective-permute-start.17 = (bf16[512,256]{1,0:T(8,128)(2,1)S(1)}, bf16[512,256]{1,0:T(8,128)(2,1)S(1)}, u32[]{:S(2)}, u32[]{:S(2)}) collective-permute-start(bf16[512,256]{1,0:T(8,128)(2,1)S(1)} %get-tuple-element.17), channel_id=1, source_target_pairs={{0,0},{64,1},{2,2},{66,3},{4,4},{68,5},{6,6},{70,7},{8,8},{72,9},{... | collective-permute-start | bytes 786440 | tf_op jit(solution)/shard_map/ppermute | solution.py:43
  221.1 8.8 %collective-permute-start.18 = (bf16[512,256]{1,0:T(8,128)(2,1)S(1)}, bf16[512,256]{1,0:T(8,128)(2,1)S(1)}, u32[]{:S(2)}, u32[]{:S(2)}) collective-permute-start(bf16[512,256]{1,0:T(8,128)(2,1)S(1)} %get-tuple-element.20), channel_id=1, source_target_pairs={{1,0},{65,1},{3,2},{67,3},{5,4},{69,5},{7,6},{71,7},{9,8},{73,9},{... | collective-permute-start | bytes 786440 | tf_op jit(solution)/shard_map/ppermute | solution.py:43
  223.8 12.5 %collective-permute-start.19 = (bf16[512,256]{1,0:T(8,128)(2,1)S(1)}, bf16[512,256]{1,0:T(8,128)(2,1)S(1)}, u32[]{:S(2)}, u32[]{:S(2)}) collective-permute-start(bf16[512,256]{1,0:T(8,128)(2,1)S(1)} %get-tuple-element.19), channel_id=1, source_target_pairs={{32,0},{96,1},{34,2},{98,3},{36,4},{100,5},{38,6},{102,7},{40,8},{... | collective-permute-start | bytes 786440 | tf_op jit(solution)/shard_map/ppermute | solution.py:43
  226.1 10.4 %collective-permute-start.20 = (bf16[512,256]{1,0:T(8,128)(2,1)S(1)}, bf16[512,256]{1,0:T(8,128)(2,1)S(1)}, u32[]{:S(2)}, u32[]{:S(2)}) collective-permute-start(bf16[512,256]{1,0:T(8,128)(2,1)S(1)} %get-tuple-element.18), channel_id=1, source_target_pairs={{33,0},{97,1},{35,2},{99,3},{37,4},{101,5},{39,6},{103,7},{41,8},{... | collective-permute-start | bytes 786440 | tf_op jit(solution)/shard_map/ppermute | solution.py:43
  236.7 6.2 %slice-start = ((s8[8388608]{0:T(1024)(128)(4,1)}), s8[4194304]{0:T(1024)(128)(4,1)S(1)}, s32[]{:S(2)}) async-start(s8[8388608]{0:T(1024)(128)(4,1)} %bitcast.121), calls=%async_computation | async-start | bytes 8388608
  236.9 6.1 %slice-start.1 = ((s8[8388608]{0:T(1024)(128)(4,1)}), s8[4194304]{0:T(1024)(128)(4,1)S(1)}, s32[]{:S(2)}) async-start(s8[8388608]{0:T(1024)(128)(4,1)} %bitcast.121), calls=%async_computation.1 | async-start | bytes 8388608
  242.9 3.1 %collective-permute-start.22 = (bf16[128,4096]{1,0:T(8,128)(2,1)S(1)}, bf16[128,4096]{1,0:T(8,128)(2,1)S(1)}, u32[]{:S(2)}, u32[]{:S(2)}) collective-permute-start(bf16[128,4096]{1,0:T(8,128)(2,1)S(1)} %dynamic-slice_bitcast_fusion), channel_id=1, source_target_pairs={{0,1},{1,0},{2,3},{3,2},{4,5},{5,4},{6,7},{7,6},{8,9},{9,8},{10,11... | collective-permute-start | bytes 3145736 | tf_op jit(solution)/shard_map/ppermute | solution.py:43
  245.4 3.2 %collective-permute-start.21 = (bf16[128,4096]{1,0:T(8,128)(2,1)S(1)}, bf16[128,4096]{1,0:T(8,128)(2,1)S(1)}, u32[]{:S(2)}, u32[]{:S(2)}) collective-permute-start(bf16[128,4096]{1,0:T(8,128)(2,1)S(1)} %dynamic-slice_bitcast_fusion.1), channel_id=1, source_target_pairs={{0,1},{1,0},{2,3},{3,2},{4,5},{5,4},{6,7},{7,6},{8,9},{9,8},{10,11... | collective-permute-start | bytes 3145736 | tf_op jit(solution)/shard_map/ppermute | solution.py:43
  246.2 26.7 %collective-permute-start.23 = (bf16[128,4096]{1,0:T(8,128)(2,1)S(1)}, bf16[128,4096]{1,0:T(8,128)(2,1)S(1)}, u32[]{:S(2)}, u32[]{:S(2)}) collective-permute-start(bf16[128,4096]{1,0:T(8,128)(2,1)S(1)} %fusion), channel_id=1, source_target_pairs={{0,2},{1,3},{2,0},{3,1},{4,6},{5,7},{6,4},{7,5},{8,10},{9,11},{10,... | collective-permute-start | bytes 3145736 | tf_op jit(solution)/shard_map/ppermute | solution.py:43
